TPU v7x, 256 devices: a whole 4x4x8 slice. The times are simulated.
256 devices in a mesh: ta: 8 (over z_lo, core), xyz: 32 (over x, y, z_hi).
Axes of the slice: x: 4, y: 4, z: 8 (z_hi: 2, z_lo: 4; z = z_hi * 4 + z_lo), core: 2. Of those that a mesh axis runs over, the one named last changes fastest.
Arguments:
- fine_field: bfloat16 [8, 128, 32, 6144], P('ta', 'xyz'), may hold values from -6 to 6
- null_vectors: bfloat16 [8, 128, 96, 6144], P('ta', 'xyz'), may hold values from -0.21875 to 0.21875
- coarse_blocks: bfloat16 [8, 128, 9, 9216], P('ta', 'xyz'), may hold values from -0.125 to 0.125
- neighbours: int32 [128, 6], replicated, may hold values from 0 to 127, as said below
- owner_map: int32 [128], replicated, may hold values from 0 to 127, as said below
Outputs:
- correction: bfloat16 [8, 128, 32, 6144], P('ta', 'xyz')
Inputs may be any that keep to these rules, and one draw needn't show every extreme that they name: Each row names six different coarse positions, the spatial neighbours of a position on a periodic lattice. The groups of four positions (4 k to 4 k + 3) form a periodic grid of 8 rows of four groups: group k lies in row k // 4 at slot k % 4. The +x and -x neighbours of a position lie in the groups of its own row whose slots follow and precede its group's slot on the cycle 0, 2, 1, 3, 0; its +y and -y neighbours lie in the groups 4 places above and below, cyclically over the 32 groups; its +z and -z neighbours lie in its own group. Each group orders its four positions as a cycle along z, in an order of its own; the x and y neighbours of a position hold the same place on their group's cycle as the position on its own. `owner_map`: A permutation of the coarse positions. The four aggregates 4 d to 4 d + 3 of the fine order go to the positions d + s * (32) for s = 0, 1, 2, 3, one each, in some order.
All inputs are finite; a program needn't handle non-finite values.
Results may differ from a plain program's by a relative error of at most 0.0085.
Values may be sent and summed in bfloat16 or wider, within the bound.
A program may use at most 64 MiB of HBM per device.

v0:
```python
import jax
import jax.numpy as jnp
from jax import lax
from jax.sharding import PartitionSpec as P

APPLIES = 3


def extended(cells, sides, width):
    for axis, dim in sides:
        count = lax.axis_size(axis)
        head = lax.slice_in_dim(cells, 0, width, axis=dim)
        tail = lax.slice_in_dim(cells, cells.shape[dim] - width, cells.shape[dim], axis=dim)
        cells = jnp.concatenate(
            [
                lax.ppermute(tail, axis, [(i, (i + 1) % count) for i in range(count)]),
                cells,
                lax.ppermute(head, axis, [((i + 1) % count, i) for i in range(count)]),
            ],
            axis=dim,
        )
    return cells


def shifted(x, axis, by):
    peers = lax.axis_size(axis)
    return lax.ppermute(x, axis, [(i, (i + by) % peers) for i in range(peers)])


def body(fine_field, null_vectors, coarse_blocks, neighbours, owner_map):
    local_sites = fine_field.shape[1]
    rhs_count = fine_field.shape[2]
    coarse_width = null_vectors.shape[2]
    packed = rhs_count * coarse_width
    all_sites = local_sites * lax.axis_size("xyz")
    first_site = lax.axis_index("xyz") * local_sites
    restricted = jnp.einsum(
        "tabk,tack->tabc", fine_field, null_vectors, preferred_element_type=jnp.float32
    )
    restricted = restricted.astype(jnp.bfloat16).reshape(1, local_sites, packed)
    targets = first_site + jnp.arange(local_sites, dtype=jnp.int32)
    piece = lax.all_gather(restricted, "xyz", axis=1, tiled=True)
    select = (owner_map[None, :] == targets[:, None]).astype(jnp.bfloat16)
    right_side = jnp.dot(select, piece[0], preferred_element_type=jnp.float32).astype(jnp.bfloat16)
    blocks = coarse_blocks.reshape(local_sites, 9, coarse_width, coarse_width)
    local_table = lax.dynamic_slice_in_dim(neighbours, first_site, local_sites, 0).reshape(-1)
    solution = right_side
    for sweep in range(APPLIES):
        slabs = extended(solution[None], (("ta", 0),), 1)
        pieces = []
        for distance in (4, 3, 2, 1, 0, -1, -2, -3, -4):
            if distance == 0:
                pieces.append(solution)
            else:
                pieces.append(shifted(solution, "xyz", distance))
        widened = jnp.concatenate(pieces, axis=0)
        below = 4
        local_label = jnp.mod(local_table - first_site + below * local_sites, all_sites)
        slot_labels = jnp.arange(widened.shape[0], dtype=jnp.int32)
        apply_select = (local_label[:, None] == slot_labels[None, :]).astype(jnp.bfloat16)
        spatial = jnp.dot(apply_select, widened, preferred_element_type=jnp.float32)
        spatial = spatial.astype(jnp.bfloat16).reshape(local_sites, 6, packed)
        stacked = jnp.concatenate(
            [solution[:, None], spatial, slabs[2][:, None], slabs[0][:, None]], axis=1
        )
        stacked = stacked.reshape(local_sites, 9, rhs_count, coarse_width)
        result = jnp.einsum("rmcn,rmbn->rbc", blocks, stacked, preferred_element_type=jnp.float32)
        solution = (right_side.astype(jnp.float32) - result.reshape(local_sites, packed)).astype(
            jnp.bfloat16
        )
    mine = lax.dynamic_slice_in_dim(owner_map, first_site, local_sites, 0)
    piece = lax.all_gather(solution[None], "xyz", axis=1, tiled=True)
    count = piece.shape[1]
    labels = jnp.arange(count, dtype=jnp.int32)
    select = (mine[:, None] == labels[None, :]).astype(jnp.bfloat16)
    back = jnp.dot(select, piece[0], preferred_element_type=jnp.float32).astype(jnp.bfloat16)
    back = back.reshape(1, local_sites, rhs_count, coarse_width)
    correction = jnp.einsum(
        "tabc,tack->tabk", back, null_vectors, preferred_element_type=jnp.float32
    )
    return correction.astype(jnp.bfloat16)


def solution(mesh):
    in_specs = (
        P("ta", "xyz", None, None),
        P("ta", "xyz", None, None),
        P("ta", "xyz", None, None),
        P(),
        P(),
    )
    out_specs = P("ta", "xyz", None, None)
    return jax.shard_map(body, mesh=mesh, in_specs=in_specs, out_specs=out_specs, check_vma=False)
```

profile of v0, /device:TPU:64, one launch (start us, length us, event | category | flops | bytes accessed | tf_op | source)
XLA Modules:
  0.0 369.4 jit_solution(17951478279362614228)
XLA Ops:
  0.0 1.4 copy-done
  1.4 4.1 %fusion.5 = bf16[4,32,96]{2,1,0:T(8,128)(2,1)S(1)} fusion(bf16[1,4,96,6144]{3,2,1,0:T(8,128)(2,1)} %param.6, bf16[1,4,32,6144]{3,2,1,0:T(8,128)(2,1)S(1)} %copy-done), kind=kOutput, calls=%fused_computation.14 | convolution fusion | flops 151007232 | bytes 6316032 | tf_op jit(solution)/shard_map/tabk,tack->tabc/dot_general | solution.py:37
  5.7 154.6 %all_gather.6 = bf16[1,128,3072]{2,0,1:T(2,128)(2,1)S(1)} all-gather(bf16[1,4,3072]{2,0,1:T(2,128)(2,1)S(1)} %reshape.105), channel_id=1, replica_groups=mesh['ta'=8,'xyz'=32] {'xyz'}, dimensions={1}, use_global_device_ids=true | all-gather | bytes 811008 | tf_op jit(solution)/shard_map/all_gather | solution.py:42
  160.9 10.1 %collective-permute-start.4 = (bf16[4,3072]{1,0:T(4,128)(2,1)S(1)}, bf16[4,3072]{1,0:T(4,128)(2,1)S(1)}, u32[]{:S(2)}, u32[]{:S(2)}) collective-permute-start(bf16[4,3072]{1,0:T(4,128)(2,1)S(1)} %convolution_convert_fusion.5), channel_id=1, source_target_pairs={{0,31},{1,0},{2,1},{3,2},{4,3},{5,4},{6,5},{7,6},{8,7},{9,8},{10,9... | collective-permute-start | bytes 73736 | tf_op jit(solution)/shard_map/ppermute | solution.py:27
  171.3 1.9 collective-permute-start.5
  173.3 6.1 %collective-permute-start.6 = (bf16[4,3072]{1,0:T(4,128)(2,1)S(1)}, bf16[4,3072]{1,0:T(4,128)(2,1)S(1)}, u32[]{:S(2)}, u32[]{:S(2)}) collective-permute-start(bf16[4,3072]{1,0:T(4,128)(2,1)S(1)} %convolution_convert_fusion.5), channel_id=1, source_target_pairs={{0,29},{1,30},{2,31},{3,0},{4,1},{5,2},{6,3},{7,4},{8,5},{9,6},{10... | collective-permute-start | bytes 73736 | tf_op jit(solution)/shard_map/ppermute | solution.py:27
  179.4 5.5 %collective-permute-start.7 = (bf16[4,3072]{1,0:T(4,128)(2,1)S(1)}, bf16[4,3072]{1,0:T(4,128)(2,1)S(1)}, u32[]{:S(2)}, u32[]{:S(2)}) collective-permute-start(bf16[4,3072]{1,0:T(4,128)(2,1)S(1)} %convolution_convert_fusion.5), channel_id=1, source_target_pairs={{0,28},{1,29},{2,30},{3,31},{4,0},{5,1},{6,2},{7,3},{8,4},{9,5},{1... | collective-permute-start | bytes 73736 | tf_op jit(solution)/shard_map/ppermute | solution.py:27
  185.1 0.7 reshape.93
  185.9 0.5 collective-permute-start.9
  187.5 1.7 collective-permute-done.9
  189.3 0.4 convolution_bitcast_fusion.2
  190.3 3.3 collective-permute-start.13
  193.5 7.0 %collective-permute-start.14 = (bf16[4,3072]{1,0:T(4,128)(2,1)S(1)}, bf16[4,3072]{1,0:T(4,128)(2,1)S(1)}, u32[]{:S(2)}, u32[]{:S(2)}) collective-permute-start(bf16[4,3072]{1,0:T(4,128)(2,1)S(1)} %fusion.36), channel_id=1, source_target_pairs={{0,31},{1,0},{2,1},{3,2},{4,3},{5,4},{6,5},{7,6},{8,7},{9,8},{10,9... | collective-permute-start | bytes 73736 | tf_op jit(solution)/shard_map/ppermute | solution.py:27
  200.5 1.9 collective-permute-start.15
  202.6 6.0 %collective-permute-start.16 = (bf16[4,3072]{1,0:T(4,128)(2,1)S(1)}, bf16[4,3072]{1,0:T(4,128)(2,1)S(1)}, u32[]{:S(2)}, u32[]{:S(2)}) collective-permute-start(bf16[4,3072]{1,0:T(4,128)(2,1)S(1)} %fusion.36), channel_id=1, source_target_pairs={{0,29},{1,30},{2,31},{3,0},{4,1},{5,2},{6,3},{7,4},{8,5},{9,6},{10... | collective-permute-start | bytes 73736 | tf_op jit(solution)/shard_map/ppermute | solution.py:27
  208.6 5.4 %collective-permute-start.17 = (bf16[4,3072]{1,0:T(4,128)(2,1)S(1)}, bf16[4,3072]{1,0:T(4,128)(2,1)S(1)}, u32[]{:S(2)}, u32[]{:S(2)}) collective-permute-start(bf16[4,3072]{1,0:T(4,128)(2,1)S(1)} %fusion.36), channel_id=1, source_target_pairs={{0,28},{1,29},{2,30},{3,31},{4,0},{5,1},{6,2},{7,3},{8,4},{9,5},{1... | collective-permute-start | bytes 73736 | tf_op jit(solution)/shard_map/ppermute | solution.py:27
  214.2 0.5 collective-permute-start.19
  214.7 0.8 collective-permute-done.17
  216.2 1.3 collective-permute-done.19
  217.6 0.4 convolution_bitcast_fusion.1
  218.3 0.9 collective-permute-start.22
  219.2 2.7 collective-permute-start.23
  221.8 7.5 %collective-permute-start.24 = (bf16[4,3072]{1,0:T(4,128)(2,1)S(1)}, bf16[4,3072]{1,0:T(4,128)(2,1)S(1)}, u32[]{:S(2)}, u32[]{:S(2)}) collective-permute-start(bf16[4,3072]{1,0:T(4,128)(2,1)S(1)} %fusion.37), channel_id=1, source_target_pairs={{0,31},{1,0},{2,1},{3,2},{4,3},{5,4},{6,5},{7,6},{8,7},{9,8},{10,9... | collective-permute-start | bytes 73736 | tf_op jit(solution)/shard_map/ppermute | solution.py:27
  229.3 1.2 collective-permute-start.25
  230.6 6.1 %collective-permute-start.26 = (bf16[4,3072]{1,0:T(4,128)(2,1)S(1)}, bf16[4,3072]{1,0:T(4,128)(2,1)S(1)}, u32[]{:S(2)}, u32[]{:S(2)}) collective-permute-start(bf16[4,3072]{1,0:T(4,128)(2,1)S(1)} %fusion.37), channel_id=1, source_target_pairs={{0,29},{1,30},{2,31},{3,0},{4,1},{5,2},{6,3},{7,4},{8,5},{9,6},{10... | collective-permute-start | bytes 73736 | tf_op jit(solution)/shard_map/ppermute | solution.py:27
  236.7 5.5 %collective-permute-start.27 = (bf16[4,3072]{1,0:T(4,128)(2,1)S(1)}, bf16[4,3072]{1,0:T(4,128)(2,1)S(1)}, u32[]{:S(2)}, u32[]{:S(2)}) collective-permute-start(bf16[4,3072]{1,0:T(4,128)(2,1)S(1)} %fusion.37), channel_id=1, source_target_pairs={{0,28},{1,29},{2,30},{3,31},{4,0},{5,1},{6,2},{7,3},{8,4},{9,5},{1... | collective-permute-start | bytes 73736 | tf_op jit(solution)/shard_map/ppermute | solution.py:27
  242.5 0.5 collective-permute-start.29
  243.0 0.7 collective-permute-done.27
  244.5 1.5 collective-permute-done.29
  246.0 0.4 convolution_bitcast_fusion
  246.6 118.0 %all-gather.1 = bf16[32,4,3072]{2,1,0:T(4,128)(2,1)S(1)} all-gather(bf16[1,4,3072]{2,1,0:T(4,128)(2,1)S(1)} %fusion.39), channel_id=2, replica_groups=mesh['ta'=8,'xyz'=32] {'xyz'}, dimensions={0}, use_global_device_ids=true | all-gather | bytes 811008 | tf_op jit(solution)/shard_map/all_gather | solution.py:72
  365.2 4.2 %fusion = bf16[1,4,32,6144]{3,2,1,0:T(8,128)(2,1)} fusion(bf16[4,32,96]{2,1,0:T(8,128)(2,1)S(1)} %reshape.97, bf16[1,4,96,6144]{3,2,1,0:T(8,128)(2,1)} %param.6), kind=kOutput, calls=%fused_computation.1 | convolution fusion | flops 151781376 | bytes 6316032 | tf_op jit(solution)/shard_map/tabc,tack->tabk/dot_general | solution.py:78
  (79 shorter events, 6.1 us)
Async XLA Ops:
  5.6 165.5 %copy-start.2 = (s32[128,6]{0,1:T(8,128)S(1)}, s32[128,6]{0,1:T(8,128)}, u32[]{:S(2)}) copy-start(s32[128,6]{0,1:T(8,128)} %param.8) | copy-start | bytes 9220
  5.6 179.5 %copy-start.1 = (bf16[1,4,9,9216]{3,1,2,0:T(4,128)(2,1)S(1)}, bf16[1,4,9,9216]{3,1,2,0:T(4,128)(2,1)}, u32[]{:S(2)}) copy-start(bf16[1,4,9,9216]{3,1,2,0:T(4,128)(2,1)} %param.7) | copy-start | bytes 1990660
  160.6 10.7 %collective-permute-start = (bf16[4,3072]{1,0:T(4,128)(2,1)S(1)}, bf16[4,3072]{1,0:T(4,128)(2,1)S(1)}, u32[]{:S(2)}, u32[]{:S(2)}) collective-permute-start(bf16[4,3072]{1,0:T(4,128)(2,1)S(1)} %convolution_convert_fusion.5), channel_id=1, source_target_pairs={{0,4},{1,5},{2,6},{3,7},{4,8},{5,9},{6,10},{7,11},{8,12},{9,13},{1... | collective-permute-start | bytes 73736 | tf_op jit(solution)/shard_map/ppermute | solution.py:27
  160.6 12.6 %collective-permute-start.1 = (bf16[4,3072]{1,0:T(4,128)(2,1)S(1)}, bf16[4,3072]{1,0:T(4,128)(2,1)S(1)}, u32[]{:S(2)}, u32[]{:S(2)}) collective-permute-start(bf16[4,3072]{1,0:T(4,128)(2,1)S(1)} %convolution_convert_fusion.5), channel_id=1, source_target_pairs={{0,3},{1,4},{2,5},{3,6},{4,7},{5,8},{6,9},{7,10},{8,11},{9,12},{10... | collective-permute-start | bytes 73736 | tf_op jit(solution)/shard_map/ppermute | solution.py:27
  160.7 18.7 %collective-permute-start.2 = (bf16[4,3072]{1,0:T(4,128)(2,1)S(1)}, bf16[4,3072]{1,0:T(4,128)(2,1)S(1)}, u32[]{:S(2)}, u32[]{:S(2)}) collective-permute-start(bf16[4,3072]{1,0:T(4,128)(2,1)S(1)} %convolution_convert_fusion.5), channel_id=1, source_target_pairs={{0,2},{1,3},{2,4},{3,5},{4,6},{5,7},{6,8},{7,9},{8,10},{9,11},{10,... | collective-permute-start | bytes 73736 | tf_op jit(solution)/shard_map/ppermute | solution.py:27
  160.8 24.9 %collective-permute-start.3 = (bf16[4,3072]{1,0:T(4,128)(2,1)S(1)}, bf16[4,3072]{1,0:T(4,128)(2,1)S(1)}, u32[]{:S(2)}, u32[]{:S(2)}) collective-permute-start(bf16[4,3072]{1,0:T(4,128)(2,1)S(1)} %convolution_convert_fusion.5), channel_id=1, source_target_pairs={{0,1},{1,2},{2,3},{3,4},{4,5},{5,6},{6,7},{7,8},{8,9},{9,10},{10,1... | collective-permute-start | bytes 73736 | tf_op jit(solution)/shard_map/ppermute | solution.py:27
  160.9 24.9 %collective-permute-start.4 = (bf16[4,3072]{1,0:T(4,128)(2,1)S(1)}, bf16[4,3072]{1,0:T(4,128)(2,1)S(1)}, u32[]{:S(2)}, u32[]{:S(2)}) collective-permute-start(bf16[4,3072]{1,0:T(4,128)(2,1)S(1)} %convolution_convert_fusion.5), channel_id=1, source_target_pairs={{0,31},{1,0},{2,1},{3,2},{4,3},{5,4},{6,5},{7,6},{8,7},{9,8},{10,9... | collective-permute-start | bytes 73736 | tf_op jit(solution)/shard_map/ppermute | solution.py:27
  171.3 15.0 %collective-permute-start.5 = (bf16[4,3072]{1,0:T(4,128)(2,1)S(1)}, bf16[4,3072]{1,0:T(4,128)(2,1)S(1)}, u32[]{:S(2)}, u32[]{:S(2)}) collective-permute-start(bf16[4,3072]{1,0:T(4,128)(2,1)S(1)} %convolution_convert_fusion.5), channel_id=1, source_target_pairs={{0,30},{1,31},{2,0},{3,1},{4,2},{5,3},{6,4},{7,5},{8,6},{9,7},{10,... | collective-permute-start | bytes 73736 | tf_op jit(solution)/shard_map/ppermute | solution.py:27
  173.3 13.1 %collective-permute-start.6 = (bf16[4,3072]{1,0:T(4,128)(2,1)S(1)}, bf16[4,3072]{1,0:T(4,128)(2,1)S(1)}, u32[]{:S(2)}, u32[]{:S(2)}) collective-permute-start(bf16[4,3072]{1,0:T(4,128)(2,1)S(1)} %convolution_convert_fusion.5), channel_id=1, source_target_pairs={{0,29},{1,30},{2,31},{3,0},{4,1},{5,2},{6,3},{7,4},{8,5},{9,6},{10... | collective-permute-start | bytes 73736 | tf_op jit(solution)/shard_map/ppermute | solution.py:27
  179.4 7.1 %collective-permute-start.7 = (bf16[4,3072]{1,0:T(4,128)(2,1)S(1)}, bf16[4,3072]{1,0:T(4,128)(2,1)S(1)}, u32[]{:S(2)}, u32[]{:S(2)}) collective-permute-start(bf16[4,3072]{1,0:T(4,128)(2,1)S(1)} %convolution_convert_fusion.5), channel_id=1, source_target_pairs={{0,28},{1,29},{2,30},{3,31},{4,0},{5,1},{6,2},{7,3},{8,4},{9,5},{1... | collective-permute-start | bytes 73736 | tf_op jit(solution)/shard_map/ppermute | solution.py:27
  185.8 1.6 collective-permute-start.8
  185.9 3.3 collective-permute-start.9
  189.8 10.7 %collective-permute-start.10 = (bf16[4,3072]{1,0:T(4,128)(2,1)S(1)}, bf16[4,3072]{1,0:T(4,128)(2,1)S(1)}, u32[]{:S(2)}, u32[]{:S(2)}) collective-permute-start(bf16[4,3072]{1,0:T(4,128)(2,1)S(1)} %fusion.36), channel_id=1, source_target_pairs={{0,4},{1,5},{2,6},{3,7},{4,8},{5,9},{6,10},{7,11},{8,12},{9,13},{1... | collective-permute-start | bytes 73736 | tf_op jit(solution)/shard_map/ppermute | solution.py:27
  189.9 12.7 %collective-permute-start.11 = (bf16[4,3072]{1,0:T(4,128)(2,1)S(1)}, bf16[4,3072]{1,0:T(4,128)(2,1)S(1)}, u32[]{:S(2)}, u32[]{:S(2)}) collective-permute-start(bf16[4,3072]{1,0:T(4,128)(2,1)S(1)} %fusion.36), channel_id=1, source_target_pairs={{0,3},{1,4},{2,5},{3,6},{4,7},{5,8},{6,9},{7,10},{8,11},{9,12},{10... | collective-permute-start | bytes 73736 | tf_op jit(solution)/shard_map/ppermute | solution.py:27
  190.2 18.4 %collective-permute-start.12 = (bf16[4,3072]{1,0:T(4,128)(2,1)S(1)}, bf16[4,3072]{1,0:T(4,128)(2,1)S(1)}, u32[]{:S(2)}, u32[]{:S(2)}) collective-permute-start(bf16[4,3072]{1,0:T(4,128)(2,1)S(1)} %fusion.36), channel_id=1, source_target_pairs={{0,2},{1,3},{2,4},{3,5},{4,6},{5,7},{6,8},{7,9},{8,10},{9,11},{10,... | collective-permute-start | bytes 73736 | tf_op jit(solution)/shard_map/ppermute | solution.py:27
  190.3 23.8 %collective-permute-start.13 = (bf16[4,3072]{1,0:T(4,128)(2,1)S(1)}, bf16[4,3072]{1,0:T(4,128)(2,1)S(1)}, u32[]{:S(2)}, u32[]{:S(2)}) collective-permute-start(bf16[4,3072]{1,0:T(4,128)(2,1)S(1)} %fusion.36), channel_id=1, source_target_pairs={{0,1},{1,2},{2,3},{3,4},{4,5},{5,6},{6,7},{7,8},{8,9},{9,10},{10,1... | collective-permute-start | bytes 73736 | tf_op jit(solution)/shard_map/ppermute | solution.py:27
  193.5 20.6 %collective-permute-start.14 = (bf16[4,3072]{1,0:T(4,128)(2,1)S(1)}, bf16[4,3072]{1,0:T(4,128)(2,1)S(1)}, u32[]{:S(2)}, u32[]{:S(2)}) collective-permute-start(bf16[4,3072]{1,0:T(4,128)(2,1)S(1)} %fusion.36), channel_id=1, source_target_pairs={{0,31},{1,0},{2,1},{3,2},{4,3},{5,4},{6,5},{7,6},{8,7},{9,8},{10,9... | collective-permute-start | bytes 73736 | tf_op jit(solution)/shard_map/ppermute | solution.py:27
  200.5 14.2 %collective-permute-start.15 = (bf16[4,3072]{1,0:T(4,128)(2,1)S(1)}, bf16[4,3072]{1,0:T(4,128)(2,1)S(1)}, u32[]{:S(2)}, u32[]{:S(2)}) collective-permute-start(bf16[4,3072]{1,0:T(4,128)(2,1)S(1)} %fusion.36), channel_id=1, source_target_pairs={{0,30},{1,31},{2,0},{3,1},{4,2},{5,3},{6,4},{7,5},{8,6},{9,7},{10,... | collective-permute-start | bytes 73736 | tf_op jit(solution)/shard_map/ppermute | solution.py:27
  202.6 12.1 %collective-permute-start.16 = (bf16[4,3072]{1,0:T(4,128)(2,1)S(1)}, bf16[4,3072]{1,0:T(4,128)(2,1)S(1)}, u32[]{:S(2)}, u32[]{:S(2)}) collective-permute-start(bf16[4,3072]{1,0:T(4,128)(2,1)S(1)} %fusion.36), channel_id=1, source_target_pairs={{0,29},{1,30},{2,31},{3,0},{4,1},{5,2},{6,3},{7,4},{8,5},{9,6},{10... | collective-permute-start | bytes 73736 | tf_op jit(solution)/shard_map/ppermute | solution.py:27
  208.6 6.9 %collective-permute-start.17 = (bf16[4,3072]{1,0:T(4,128)(2,1)S(1)}, bf16[4,3072]{1,0:T(4,128)(2,1)S(1)}, u32[]{:S(2)}, u32[]{:S(2)}) collective-permute-start(bf16[4,3072]{1,0:T(4,128)(2,1)S(1)} %fusion.36), channel_id=1, source_target_pairs={{0,28},{1,29},{2,30},{3,31},{4,0},{5,1},{6,2},{7,3},{8,4},{9,5},{1... | collective-permute-start | bytes 73736 | tf_op jit(solution)/shard_map/ppermute | solution.py:27
  214.1 2.0 collective-permute-start.18
  214.2 3.3 collective-permute-start.19
  218.1 11.2 %collective-permute-start.20 = (bf16[4,3072]{1,0:T(4,128)(2,1)S(1)}, bf16[4,3072]{1,0:T(4,128)(2,1)S(1)}, u32[]{:S(2)}, u32[]{:S(2)}) collective-permute-start(bf16[4,3072]{1,0:T(4,128)(2,1)S(1)} %fusion.37), channel_id=1, source_target_pairs={{0,4},{1,5},{2,6},{3,7},{4,8},{5,9},{6,10},{7,11},{8,12},{9,13},{1... | collective-permute-start | bytes 73736 | tf_op jit(solution)/shard_map/ppermute | solution.py:27
  218.2 12.4 %collective-permute-start.21 = (bf16[4,3072]{1,0:T(4,128)(2,1)S(1)}, bf16[4,3072]{1,0:T(4,128)(2,1)S(1)}, u32[]{:S(2)}, u32[]{:S(2)}) collective-permute-start(bf16[4,3072]{1,0:T(4,128)(2,1)S(1)} %fusion.37), channel_id=1, source_target_pairs={{0,3},{1,4},{2,5},{3,6},{4,7},{5,8},{6,9},{7,10},{8,11},{9,12},{10... | collective-permute-start | bytes 73736 | tf_op jit(solution)/shard_map/ppermute | solution.py:27
  218.3 18.4 %collective-permute-start.22 = (bf16[4,3072]{1,0:T(4,128)(2,1)S(1)}, bf16[4,3072]{1,0:T(4,128)(2,1)S(1)}, u32[]{:S(2)}, u32[]{:S(2)}) collective-permute-start(bf16[4,3072]{1,0:T(4,128)(2,1)S(1)} %fusion.37), channel_id=1, source_target_pairs={{0,2},{1,3},{2,4},{3,5},{4,6},{5,7},{6,8},{7,9},{8,10},{9,11},{10,... | collective-permute-start | bytes 73736 | tf_op jit(solution)/shard_map/ppermute | solution.py:27
  219.2 23.3 %collective-permute-start.23 = (bf16[4,3072]{1,0:T(4,128)(2,1)S(1)}, bf16[4,3072]{1,0:T(4,128)(2,1)S(1)}, u32[]{:S(2)}, u32[]{:S(2)}) collective-permute-start(bf16[4,3072]{1,0:T(4,128)(2,1)S(1)} %fusion.37), channel_id=1, source_target_pairs={{0,1},{1,2},{2,3},{3,4},{4,5},{5,6},{6,7},{7,8},{8,9},{9,10},{10,1... | collective-permute-start | bytes 73736 | tf_op jit(solution)/shard_map/ppermute | solution.py:27
  221.8 20.7 %collective-permute-start.24 = (bf16[4,3072]{1,0:T(4,128)(2,1)S(1)}, bf16[4,3072]{1,0:T(4,128)(2,1)S(1)}, u32[]{:S(2)}, u32[]{:S(2)}) collective-permute-start(bf16[4,3072]{1,0:T(4,128)(2,1)S(1)} %fusion.37), channel_id=1, source_target_pairs={{0,31},{1,0},{2,1},{3,2},{4,3},{5,4},{6,5},{7,6},{8,7},{9,8},{10,9... | collective-permute-start | bytes 73736 | tf_op jit(solution)/shard_map/ppermute | solution.py:27
  229.3 13.7 %collective-permute-start.25 = (bf16[4,3072]{1,0:T(4,128)(2,1)S(1)}, bf16[4,3072]{1,0:T(4,128)(2,1)S(1)}, u32[]{:S(2)}, u32[]{:S(2)}) collective-permute-start(bf16[4,3072]{1,0:T(4,128)(2,1)S(1)} %fusion.37), channel_id=1, source_target_pairs={{0,30},{1,31},{2,0},{3,1},{4,2},{5,3},{6,4},{7,5},{8,6},{9,7},{10,... | collective-permute-start | bytes 73736 | tf_op jit(solution)/shard_map/ppermute | solution.py:27
  230.6 12.5 %collective-permute-start.26 = (bf16[4,3072]{1,0:T(4,128)(2,1)S(1)}, bf16[4,3072]{1,0:T(4,128)(2,1)S(1)}, u32[]{:S(2)}, u32[]{:S(2)}) collective-permute-start(bf16[4,3072]{1,0:T(4,128)(2,1)S(1)} %fusion.37), channel_id=1, source_target_pairs={{0,29},{1,30},{2,31},{3,0},{4,1},{5,2},{6,3},{7,4},{8,5},{9,6},{10... | collective-permute-start | bytes 73736 | tf_op jit(solution)/shard_map/ppermute | solution.py:27
  236.7 7.1 %collective-permute-start.27 = (bf16[4,3072]{1,0:T(4,128)(2,1)S(1)}, bf16[4,3072]{1,0:T(4,128)(2,1)S(1)}, u32[]{:S(2)}, u32[]{:S(2)}) collective-permute-start(bf16[4,3072]{1,0:T(4,128)(2,1)S(1)} %fusion.37), channel_id=1, source_target_pairs={{0,28},{1,29},{2,30},{3,31},{4,0},{5,1},{6,2},{7,3},{8,4},{9,5},{1... | collective-permute-start | bytes 73736 | tf_op jit(solution)/shard_map/ppermute | solution.py:27
  242.4 2.0 collective-permute-start.28
  242.5 3.4 collective-permute-start.29
  (2 other events, 156.2 us)
where the time goes:
time: 370 us; the launch traced here: 369 us
  blocking collectives  273 us (74%)
  starting transfers between devices  73.9 us (20%)
  matrix products  10.8 us (3%)
  waiting for transfers between devices  6.62 us (2%)
  local copies, waits for them, and re-layouts  5.09 us (1%)
    all_gather x1, blocking collectives, body(): piece = lax.all_gather(restricted, 'xyz', axis=1, tiled=True)  155 us
    all_gather x1, blocking collectives, body(): piece = lax.all_gather(solution[None], 'xyz', axis=1, tiled=True)  118 us
    ppermute x24, starting transfers between devices, shifted(): return lax.ppermute(x, axis, [(i, (i + by) % peers) for i in range(peers)])  72.1 us
  transfers between devices with their start and end apart: 30, of which 8 were waited for; matrix products, arithmetic and copies ran while one was open for 1% of the time, Pallas kernels for 0%

commit v1 on v0

v1 whole, which is shorter than its diff:
```python
import jax
import jax.numpy as jnp
from jax import lax
from jax.experimental import pallas as pl
from jax.experimental.pallas import tpu as pltpu
from jax.sharding import PartitionSpec as P

MESH = pl.DeviceIdType.MESH
APPLIES = 3
SITES = 4
NRHS = 32
NC = 96
LANES = 128
KF = 6144
CUTS = 2
PIECE = KF // CUTS
OUT_PIECE = 1024
NT = (((1,), (1,)), ((), ()))


def dot_nt(a, b):
    return lax.dot_general(a, b, NT, preferred_element_type=jnp.float32)


def kernel(
    fine_hbm, null_hbm, blocks_hbm, neighbours, owner_map, out_hbm,
    fine, null, blocks, weights, out, rest, outgoing, rhs, fields, halos, returned,
    load_sem, block_sem, out_sem, go_send, go_recv, halo_send, halo_recv, back_send, back_recv,
):
    t = lax.axis_index("ta")
    d = lax.axis_index("xyz")

    dests = [d // 4 + 8 * s for s in range(4)]
    sources = [4 * (d % 8) + j for j in range(4)]
    slot = d % 4
    across = (slot % 2) * 2 + slot // 2
    after, before = (across + 1) % 4, (across + 3) % 4
    row = d - slot
    x_up = row + (after % 2) * 2 + after // 2
    x_down = row + (before % 2) * 2 + before // 2
    y_up, y_down = (d + 4) % 32, (d + 28) % 32
    t_up, t_down = (t + 1) % 8, (t + 7) % 8
    sides = [
        ((t, x_down), 1), ((t, x_up), 2),
        ((t, y_down), 3), ((t, y_up), 4),
        ((t_down, d), 7), ((t_up, d), 8),
    ]

    loads = []
    for a in range(SITES):
        for c in range(CUTS):
            part = pl.ds(c * PIECE, PIECE)
            pair = [
                pltpu.make_async_copy(
                    fine_hbm.at[a, :, part], fine.at[a, :, part], load_sem.at[0, a * CUTS + c]
                ),
                pltpu.make_async_copy(
                    null_hbm.at[a, :, part], null.at[a, :, part], load_sem.at[1, a * CUTS + c]
                ),
            ]
            for copy in pair:
                copy.start()
            loads.append(pair)
    load_blocks = pltpu.make_async_copy(blocks_hbm, blocks, block_sem)
    load_blocks.start()

    barrier = pltpu.get_barrier_semaphore()
    for (to_t, to_d), _ in sides:
        pl.semaphore_signal(barrier, inc=1, device_id=(to_t, to_d), device_id_type=MESH)
    for partner in dests + sources:
        @pl.when(partner != d)
        def _():
            pl.semaphore_signal(barrier, inc=1, device_id=(t, partner), device_id_type=MESH)

    for ref in [rest] + list(fields):
        ref[...] = jnp.zeros_like(ref)
    weights[...] = jnp.zeros_like(weights)

    for a in range(SITES):
        total = jnp.zeros((NRHS, NC), jnp.float32)
        for c in range(CUTS):
            for copy in loads[a * CUTS + c]:
                copy.wait()
            part = pl.ds(c * PIECE, PIECE)
            total += dot_nt(fine[a, :, part], null[a, :, part])
        rest[a, :, :NC] = total.astype(jnp.bfloat16)

    strides = [owner_map[4 * d + a] // 32 for a in range(SITES)]
    for s in range(4):
        chosen = 0
        for a in range(1, SITES):
            chosen = jnp.where(strides[a] == s, a, chosen)
        outgoing[s] = rest[chosen]

    own = 0
    for partner in dests:
        own = own + jnp.where(partner == d, 1, 0)
    pl.semaphore_wait(barrier, 6 + 8 - 2 * own)

    def go(s):
        return pltpu.make_async_remote_copy(
            src_ref=outgoing.at[s], dst_ref=rhs.at[slot],
            send_sem=go_send.at[s], recv_sem=go_recv.at[slot],
            device_id=(t, dests[s]), device_id_type=MESH,
        )

    def arrived(j):
        return pltpu.make_async_remote_copy(
            src_ref=outgoing.at[j], dst_ref=rhs.at[j],
            send_sem=go_send.at[j], recv_sem=go_recv.at[j],
            device_id=(t, d), device_id_type=MESH,
        )

    for s in range(4):
        @pl.when(dests[s] != d)
        def _():
            go(s).start()

        @pl.when(dests[s] == d)
        def _():
            rhs[slot] = outgoing[s]

    load_blocks.wait()
    for s in range(SITES):
        for m in range(9):
            weights[s, :, m * LANES : m * LANES + NC] = blocks[m, s]

    for j in range(4):
        @pl.when(sources[j] != d)
        def _():
            arrived(j).wait_recv()

    places = [[neighbours[c, 4 * d + s] % 4 for c in range(6)] for s in range(SITES)]
    for k in range(APPLIES):
        field = rhs if k == 0 else fields[k - 1]
        copies = {}
        for i, ((to_t, to_d), m) in enumerate(sides):
            copies[m] = pltpu.make_async_remote_copy(
                src_ref=field, dst_ref=halos[6 * k + i],
                send_sem=halo_send.at[k, i], recv_sem=halo_recv.at[k, i],
                device_id=(to_t, to_d), device_id_type=MESH,
            )
            copies[m].start()

        def piece(s, ms, inputs):
            total = None
            for m, x in zip(ms, inputs):
                term = dot_nt(x, weights[s, :, m * LANES : (m + 1) * LANES])
                total = term if total is None else total + term
            return total

        totals = [
            piece(s, (0, 5, 6), (field[s], field[places[s][4]], field[places[s][5]]))
            for s in range(SITES)
        ]
        for ms in ((7, 8), (3, 4), (1, 2)):
            for m in ms:
                copies[m].wait_recv()
            first = halos[6 * k + [side[1] for side in sides].index(ms[0])]
            second = halos[6 * k + [side[1] for side in sides].index(ms[1])]
            for s in range(SITES):
                if ms[0] == 7:
                    pair = (first[s], second[s])
                else:
                    pair = (first[places[s][ms[0] - 1]], second[places[s][ms[1] - 1]])
                totals[s] = totals[s] + piece(s, ms, pair)
        for s in range(SITES):
            new = rhs[s, :, :NC].astype(jnp.float32) - totals[s]
            fields[k][s, :, :NC] = new.astype(jnp.bfloat16)
        for copy in copies.values():
            copy.wait_send()

    answer = fields[APPLIES - 1]
    stride = d // 8

    def come(j):
        return pltpu.make_async_remote_copy(
            src_ref=answer.at[j], dst_ref=returned.at[stride],
            send_sem=back_send.at[j], recv_sem=back_recv.at[stride],
            device_id=(t, sources[j]), device_id_type=MESH,
        )

    def came(s):
        return pltpu.make_async_remote_copy(
            src_ref=answer.at[s], dst_ref=returned.at[s],
            send_sem=back_send.at[s], recv_sem=back_recv.at[s],
            device_id=(t, d), device_id_type=MESH,
        )

    for j in range(4):
        @pl.when(sources[j] != d)
        def _():
            come(j).start()

        @pl.when(sources[j] == d)
        def _():
            returned[stride] = answer[j]
    for s in range(4):
        @pl.when(dests[s] != d)
        def _():
            go(s).wait_send()
            came(s).wait_recv()

    stores = []
    for a in range(SITES):
        back = returned[strides[a]][:, :NC]
        for c in range(KF // OUT_PIECE):
            part = pl.ds(c * OUT_PIECE, OUT_PIECE)
            out[a, :, part] = jnp.dot(
                back, null[a, :, part], preferred_element_type=jnp.float32
            ).astype(jnp.bfloat16)
        copy = pltpu.make_async_copy(out.at[a], out_hbm.at[a], out_sem.at[a])
        copy.start()
        stores.append(copy)
    for j in range(4):
        @pl.when(sources[j] != d)
        def _():
            come(j).wait_send()
    for copy in stores:
        copy.wait()


def body(fine_field, null_vectors, coarse_blocks, neighbours, owner_map):
    blocks = coarse_blocks.reshape(SITES, 9, NC, NC).transpose(1, 0, 2, 3)
    hbm = pl.BlockSpec(memory_space=pl.ANY)
    smem = pl.BlockSpec(memory_space=pltpu.SMEM)
    field = pltpu.VMEM((SITES, NRHS, LANES), jnp.bfloat16)
    dma = pltpu.SemaphoreType.DMA
    result = pl.pallas_call(
        kernel,
        out_shape=jax.ShapeDtypeStruct((SITES, NRHS, KF), jnp.bfloat16),
        in_specs=[hbm, hbm, hbm, smem, smem],
        out_specs=hbm,
        scratch_shapes=[
            pltpu.VMEM((SITES, NRHS, KF), jnp.bfloat16),
            pltpu.VMEM((SITES, NC, KF), jnp.bfloat16),
            pltpu.VMEM((9, SITES, NC, NC), jnp.bfloat16),
            pltpu.VMEM((SITES, NC, 9 * LANES), jnp.bfloat16),
            pltpu.VMEM((SITES, NRHS, KF), jnp.bfloat16),
            field, field, field,
            [field] * APPLIES,
            [field] * (6 * APPLIES),
            field,
            dma((2, SITES * CUTS)), dma, dma((SITES,)),
            dma((4,)), dma((4,)),
            dma((APPLIES, 6)), dma((APPLIES, 6)),
            dma((4,)), dma((4,)),
        ],
        compiler_params=pltpu.CompilerParams(
            collective_id=0, has_side_effects=True, vmem_limit_bytes=40 * 1024 * 1024
        ),
    )(fine_field[0], null_vectors[0], blocks, neighbours.T, owner_map)
    return result[None]


def solution(mesh):
    in_specs = (
        P("ta", "xyz", None, None),
        P("ta", "xyz", None, None),
        P("ta", "xyz", None, None),
        P(),
        P(),
    )
    out_specs = P("ta", "xyz", None, None)
    return jax.shard_map(body, mesh=mesh, in_specs=in_specs, out_specs=out_specs, check_vma=False)
```

time: 370 us -> 52.6 us (0.14)
  the two profiles are of different devices: /device:TPU:64 before, /device:TPU:16 now
where the time goes in v1:
time: 52.6 us; the launch traced here: 52.4 us
  Pallas kernels  44.2 us (84%)
  local copies, waits for them, and re-layouts  8.2 us (16%)
    pallas_call x1, Pallas kernels, body(): pl.pallas_call(kernel, out_shape=jax.ShapeDtypeStruct((SITES, NRHS, KF),...  44.2 us
    unnamed x9, local copies, waits for them, and re-layouts  6.23 us
    reshape x1, local copies, waits for them, and re-layouts, body(): blocks = coarse_blocks.reshape(SITES, 9, NC, NC).transpose(1, 0, 2, 3)  1.97 us

profile of v1, /device:TPU:16, one launch (start us, length us, event | category | flops | bytes accessed | tf_op | source)
XLA Modules:
  0.0 52.4 jit_solution(5619671415886176342)
XLA Ops:
  0.0 2.0 %reshape.3 = bf16[4,9,96,96]{3,2,0,1:T(8,128)(2,1)S(1)} reshape(bf16[1,4,9,9216]{3,1,2,0:T(4,128)(2,1)} %param.7) | data formatting | bytes 1327104 | tf_op jit(solution)/shard_map/reshape | solution.py:224
  2.0 0.0 copy-start
  2.0 2.3 %copy-done = bf16[1,4,96,6144]{3,2,1,0:T(8,128)(2,1)S(1)} copy-done((bf16[1,4,96,6144]{3,2,1,0:T(8,128)(2,1)S(1)}, bf16[1,4,96,6144]{3,2,1,0:T(8,128)(2,1)}, u32[]{:S(2)}) %copy-start) | copy-done | bytes 4718616
  4.3 0.0 copy-start.1
  4.3 1.4 %copy-done.1 = bf16[1,4,32,6144]{3,2,1,0:T(8,128)(2,1)S(1)} copy-done((bf16[1,4,32,6144]{3,2,1,0:T(8,128)(2,1)S(1)}, bf16[1,4,32,6144]{3,2,1,0:T(8,128)(2,1)}, u32[]{:S(2)}) %copy-start.1) | copy-done | bytes 1572888
  5.7 0.0 copy-start.2
  5.7 0.7 %copy-done.2 = s32[128,6]{0,1:T(8,128)S(1)} copy-done((s32[128,6]{0,1:T(8,128)S(1)}, s32[128,6]{0,1:T(8,128)}, u32[]{:S(2)}) %copy-start.2) | copy-done | bytes 3096
  6.4 0.0 copy-start.3
  6.4 0.7 %copy-done.3 = s32[128]{0:T(128)S(1)} copy-done((s32[128]{0:T(128)S(1)}, s32[128]{0:T(128)}, u32[]{:S(2)}) %copy-start.3) | copy-done | bytes 536
  7.1 44.2 %shard_map.55 = bf16[4,32,6144]{2,1,0:T(8,128)(2,1)S(1)} custom-call(bf16[4,32,6144]{2,1,0:T(8,128)(2,1)S(1)} %bitcast.10, bf16[4,96,6144]{2,1,0:T(8,128)(2,1)S(1)} %bitcast.8, bf16[9,4,96,96]{3,2,1,0:T(8,128)(2,1)S(1)} %bitcast.9, s32[6,128]{1,0:T(8,128)S(1)} %bitcast.11, s32[128]{0:T(128)S(1)} %copy-done.3), custom_call_target="tpu_custom_call" | custom-call | tf_op jit(solution)/shard_map/pallas_call | solution.py:229
  51.3 1.1 %copy.7 = bf16[1,4,32,6144]{3,2,1,0:T(8,128)(2,1)} copy(bf16[1,4,32,6144]{3,2,1,0:T(8,128)(2,1)S(1)} %bitcast.7) | data formatting | bytes 3145728
Async XLA Ops:
  2.0 2.3 %copy-start = (bf16[1,4,96,6144]{3,2,1,0:T(8,128)(2,1)S(1)}, bf16[1,4,96,6144]{3,2,1,0:T(8,128)(2,1)}, u32[]{:S(2)}) copy-start(bf16[1,4,96,6144]{3,2,1,0:T(8,128)(2,1)} %param.6) | copy-start | bytes 14155780
  4.3 1.4 %copy-start.1 = (bf16[1,4,32,6144]{3,2,1,0:T(8,128)(2,1)S(1)}, bf16[1,4,32,6144]{3,2,1,0:T(8,128)(2,1)}, u32[]{:S(2)}) copy-start(bf16[1,4,32,6144]{3,2,1,0:T(8,128)(2,1)} %param.5) | copy-start | bytes 4718596
  5.7 0.7 %copy-start.2 = (s32[128,6]{0,1:T(8,128)S(1)}, s32[128,6]{0,1:T(8,128)}, u32[]{:S(2)}) copy-start(s32[128,6]{0,1:T(8,128)} %param.8) | copy-start | bytes 9220
  6.4 0.7 %copy-start.3 = (s32[128]{0:T(128)S(1)}, s32[128]{0:T(128)}, u32[]{:S(2)}) copy-start(s32[128]{0:T(128)} %owner_map.1) | copy-start | bytes 1540
